TPU v7x, 32 devices: a whole 2x2x4 slice. The times are simulated.
32 devices in a mesh: row: 8 (over y, x, core), col: 4 (over z).
Axes of the slice: x: 2, y: 2, z: 4, core: 2. Of those that a mesh axis runs over, the one named last changes fastest.
Arguments:
- tokens: bfloat16 [8, 4, 736, 1024], P('row', 'col'), may hold values from -6 to 6
- local_params: bfloat16 [8, 4, 2, 1024, 1024], P('row', 'col'), may hold values from -0.1875 to 0.1875
- outer_params: float32 [2, 4, 4, 8, 32, 1024], P(None, None, 'col', 'row'), may hold values from -0.1875 to 0.1875
- momentum: float32 [2, 4, 4, 8, 32, 1024], P(None, None, 'col', 'row'), may hold values from -0.1875 to 0.1875
- table: int32 [8, 4], replicated, may hold values from 0 to 3, each once within a row
- counts: int32 [8, 4], replicated, may hold values from 64 to 4095
Outputs:
- path_params: bfloat16 [8, 4, 2, 1024, 1024], P('row', 'col')
- outer_out: float32 [2, 4, 4, 8, 32, 1024], P(None, None, 'col', 'row')
- momentum_out: float32 [2, 4, 4, 8, 32, 1024], P(None, None, 'col', 'row')
- hidden_out: bfloat16 [8, 4, 736, 1024], P('row', 'col')
Inputs may be any that keep to these rules, and one draw needn't show every extreme that they name: Each row of the table names every level-two module exactly once.
All inputs are finite; a program needn't handle non-finite values.
Results may differ from a plain program's by a relative error of at most 0.01.
Values may be sent and summed in bfloat16 or wider, within the bound.
A program may use at most 64 MiB of HBM per device.

v0:
```python
import jax
import jax.numpy as jnp
from jax import lax
from jax.sharding import PartitionSpec as P


def outer_round(scaled, outer, moment, my_row, inverse):
    layers = scaled.shape[0]
    width = scaled.shape[-1]
    n_col = lax.axis_size("col")
    n_row = lax.axis_size("row")
    pieces = scaled.reshape(layers, n_col, width // n_col, width)
    arrived = lax.all_to_all(pieces, "col", split_axis=1, concat_axis=1, tiled=True)
    ordered = jnp.take(arrived, inverse, axis=1)
    split = ordered.reshape(layers, n_col, n_row, width // (n_col * n_row), width)
    landed = lax.all_to_all(split, "row", split_axis=2, concat_axis=2, tiled=True)
    summed = jnp.sum(landed.astype(jnp.float32), axis=2)
    delta = outer - summed
    moment_new = 0.9 * moment + delta
    outer_new = outer - 0.7 * (delta + 0.9 * moment_new)
    whole = lax.all_gather(outer_new.astype(jnp.bfloat16), "row", axis=2, tiled=True)
    chosen = jnp.take(whole, my_row, axis=1)
    returned = lax.all_to_all(chosen, "col", split_axis=1, concat_axis=1, tiled=True)
    return (outer_new, moment_new, returned.reshape(layers, width, width))


def micro_step(tokens_path, params_path):
    state = tokens_path.astype(jnp.float32)
    for layer in range(params_path.shape[0]):
        scale = lax.rsqrt(jnp.mean(state * state, axis=-1, keepdims=True) + 1e-06)
        normed = (state * scale).astype(jnp.bfloat16)
        mixed = jnp.dot(normed, params_path[layer], preferred_element_type=jnp.float32)
        state = state + jax.nn.gelu(mixed, approximate=False)
    return state.astype(jnp.bfloat16)


def on_device(tokens, local_params, outer_params, momentum, table, counts):
    row_index = lax.axis_index("row")
    col_index = lax.axis_index("col")
    n_col = table.shape[1]
    ids = jnp.arange(n_col, dtype=jnp.int32)
    matches = (table[:, :, None] == ids[None, None, :]).astype(jnp.float32)
    totals = jnp.sum(counts.astype(jnp.float32)[:, :, None] * matches, axis=(0, 1))
    my_row = lax.dynamic_index_in_dim(table, row_index, 0, keepdims=False)
    count_row = lax.dynamic_index_in_dim(counts, row_index, 0, keepdims=False)
    my_module = lax.dynamic_index_in_dim(my_row, col_index, 0, keepdims=False)
    my_count = lax.dynamic_index_in_dim(count_row, col_index, 0, keepdims=False)
    share = my_count.astype(jnp.float32) / jnp.sum(totals * (ids == my_module).astype(jnp.float32))
    inverse = jnp.sum(ids[:, None] * (my_row[:, None] == ids[None, :]).astype(jnp.int32), axis=0)
    params = local_params[0, 0]
    layers = params.shape[0]
    width = params.shape[-1]
    scaled = (share * params.astype(jnp.float32)).astype(jnp.bfloat16)
    outer = outer_params.reshape(layers, n_col, -1, width)
    moment = momentum.reshape(layers, n_col, -1, width)
    outer_new, moment_new, returned = outer_round(scaled, outer, moment, my_row, inverse)
    hidden = micro_step(tokens[0, 0], params)
    return (
        returned[None, None],
        outer_new.reshape(outer_params.shape),
        moment_new.reshape(momentum.shape),
        hidden[None, None],
    )


def solution(mesh):
    return jax.shard_map(
        on_device,
        mesh=mesh,
        in_specs=(
            P("row", "col", None, None),
            P("row", "col", None, None, None),
            P(None, None, "col", "row", None, None),
            P(None, None, "col", "row", None, None),
            P(),
            P(),
        ),
        out_specs=(
            P("row", "col", None, None, None),
            P(None, None, "col", "row", None, None),
            P(None, None, "col", "row", None, None),
            P("row", "col", None, None),
        ),
        check_vma=False,
    )
```

profile of v0, /device:TPU:15, one launch (start us, length us, event | category | flops | bytes accessed | tf_op | source)
XLA Modules:
  0.0 331.5 jit_solution(18327795079356649109)
XLA Ops:
  7.2 0.7 convert_element_type.53
  7.9 1.3 dynamic_slice.12
  9.1 1.3 dynamic_slice.13
  10.4 0.8 select_reduce_fusion
  11.8 1.2 fusion.51
  13.8 3.3 multiply_convert_fusion
  17.1 2.5 copy.53
  19.5 5.1 %all-to-all-start = ((bf16[2,4,256,1024]{3,2,0,1:T(8,128)(2,1)}), bf16[2,4,256,1024]{3,2,0,1:T(8,128)(2,1)}, u32[]{:S(2)}, u32[]{:S(2)}) async-start(bf16[2,4,256,1024]{3,2,0,1:T(8,128)(2,1)} %copy.53), calls=%async_computation | async-start | bytes 8388608 | tf_op jit(solution)/shard_map/all_to_all | solution.py:13
  24.6 0.0 all-gather.2.cloned.1.call-start
  24.6 0.2 dynamic-slice_reduce_fusion
  24.8 0.1 select_reduce_fusion.1
  24.9 89.2 %all-to-all-done = bf16[2,4,256,1024]{3,2,0,1:T(8,128)(2,1)} async-done(((bf16[2,4,256,1024]{3,2,0,1:T(8,128)(2,1)}), bf16[2,4,256,1024]{3,2,0,1:T(8,128)(2,1)}, u32[]{:S(2)}, u32[]{:S(2)}) %all-to-all-start) | async-done | bytes 4194336 | tf_op jit(solution)/shard_map/all_to_all | solution.py:13
  114.1 5.0 %gather_fusion = bf16[4,2,256,1024]{3,2,1,0:T(8,128)(2,1)} fusion(bf16[2,4,256,1024]{3,2,0,1:T(8,128)(2,1)} %all-to-all-done, s32[1024]{0:T(1024)S(1)} %pad_clamp_fusion.1), kind=kCustom, calls=%fused_computation.clone | custom fusion | bytes 8388624 | tf_op jit(solution)/shard_map/jit(_take)/gather | solution.py:14
  119.1 2.7 broadcast_select_fusion
  121.8 0.8 copy.54
  122.6 51.6 %all_to_all.15 = bf16[2,4,8,32,1024]{4,3,0,1,2:T(8,128)(2,1)S(1)} all-to-all(bf16[2,4,8,32,1024]{4,3,0,1,2:T(8,128)(2,1)S(1)} %copy.54), channel_id=1, replica_groups=mesh['row'=8,'col'=4] {'row'}, dimensions={2} | all-to-all | bytes 8388608 | tf_op jit(solution)/shard_map/all_to_all | solution.py:16
  174.2 0.9 convert_reduce_fusion
  175.1 0.3 copy-done
  175.4 0.3 copy-done.1
  175.7 1.2 fusion.48
  176.9 0.0 all-gather.2.cloned.1.call-update
  177.0 38.3 %all-gather.2.cloned.1.call-done = bf16[2,4,256,1024]{3,2,1,0:T(8,128)(2,1)} async-done(((bf16[2,4,32,1024]{3,2,1,0:T(8,128)(2,1)}), bf16[2,4,256,1024]{3,2,1,0:T(8,128)(2,1)}) %all-gather.2.cloned.1.call-update) | async-done | bytes 4194320 | tf_op jit(solution)/shard_map/all_gather | solution.py:21
  215.2 5.0 %gather_fusion.1 = bf16[4,2,256,1024]{3,2,1,0:T(8,128)(2,1)} fusion(bf16[2,4,256,1024]{3,2,1,0:T(8,128)(2,1)} %all-gather.2.cloned.1.call-done, s32[1024]{0:T(1024)S(1)} %pad_clamp_fusion), kind=kCustom, calls=%fused_computation.1.clone | custom fusion | bytes 8388624 | tf_op jit(solution)/shard_map/jit(_take)/gather | solution.py:22
  220.2 4.7 %select_bitcast_fusion = bf16[2,4,256,1024]{3,2,0,1:T(8,128)(2,1)} fusion(bf16[4,2,256,1024]{3,2,1,0:T(8,128)(2,1)} %gather_fusion.1, pred[4]{0:T(512)(128)(4,1)S(1)} %compare_and_fusion), kind=kLoop, calls=%fused_computation.6 | loop fusion | flops 2097152 | bytes 8388612 | tf_op jit(solution)/shard_map/jit(_take)/select_n | solution.py:22
  224.9 5.1 %all-to-all-start.2 = ((bf16[2,4,256,1024]{3,2,0,1:T(8,128)(2,1)}), bf16[2,4,256,1024]{3,2,0,1:T(8,128)(2,1)}, u32[]{:S(2)}, u32[]{:S(2)}) async-start(bf16[2,4,256,1024]{3,2,0,1:T(8,128)(2,1)} %select_bitcast_fusion), calls=%async_computation.2 | async-start | bytes 8388608 | tf_op jit(solution)/shard_map/all_to_all | solution.py:23
  230.0 1.7 fusion.2
  231.8 0.0 copy-start.2
  231.8 10.9 %multiply_reduce_fusion = (f32[736]{0:T(1024)S(1)}, f32[736,1024]{1,0:T(8,128)S(1)}) fusion(bf16[1,1,2,1024,1024]{4,3,2,1,0:T(8,128)(2,1)} %param.9, bf16[1,1,736,1024]{3,2,1,0:T(8,128)(2,1)} %param.8, f32[736]{0:T(1024)S(1)} %add_rsqrt_fusion.1), kind=kOutput, calls=%fused_computation.34 | convolution fusion | flops 1597013248 | bytes 8132352 | tf_op jit(solution)/shard_map/dot_general | solution.py:32
  242.7 9.4 %fusion.36 = bf16[1,1,736,1024]{3,2,1,0:T(8,128)(2,1)} fusion(f32[736,1024]{1,0:T(8,128)S(1)} %get-tuple-element.24, bf16[1,1,2,1024,1024]{4,3,2,1,0:T(8,128)(2,1)S(1)} %copy-done.2, f32[736]{0:T(1024)S(1)} %add_rsqrt_fusion), kind=kOutput, calls=%fused_computation.61 | convolution fusion | flops 1594753024 | bytes 9637888 | tf_op jit(solution)/shard_map/dot_general | solution.py:32
  252.1 1.7 fusion.50
  253.8 66.2 %all-to-all-done.2 = bf16[2,4,256,1024]{3,2,0,1:T(8,128)(2,1)} async-done(((bf16[2,4,256,1024]{3,2,0,1:T(8,128)(2,1)}), bf16[2,4,256,1024]{3,2,0,1:T(8,128)(2,1)}, u32[]{:S(2)}, u32[]{:S(2)}) %all-to-all-start.2) | async-done | bytes 4194336 | tf_op jit(solution)/shard_map/all_to_all | solution.py:23
  320.0 4.6 %copy.58 = bf16[2,4,256,1024]{3,2,1,0:T(8,128)(2,1)} copy(bf16[2,4,256,1024]{3,2,0,1:T(8,128)(2,1)} %all-to-all-done.2) | data formatting | bytes 8388608 | tf_op jit(solution)/shard_map/all_to_all | solution.py:23
  (13 shorter events, 0.1 us)
Async XLA Ops:
  19.5 5.1 %copy-start.3 = (s32[8,4]{0,1:T(4,128)S(1)}, s32[8,4]{0,1:T(4,128)}, u32[]{:S(2)}) copy-start(s32[8,4]{0,1:T(4,128)} %param.12) | copy-start | bytes 388
  19.5 94.6 %all-to-all-start = ((bf16[2,4,256,1024]{3,2,0,1:T(8,128)(2,1)}), bf16[2,4,256,1024]{3,2,0,1:T(8,128)(2,1)}, u32[]{:S(2)}, u32[]{:S(2)}) async-start(bf16[2,4,256,1024]{3,2,0,1:T(8,128)(2,1)} %copy.53), calls=%async_computation | async-start | bytes 8388608 | tf_op jit(solution)/shard_map/all_to_all | solution.py:13
  24.6 190.6 %all-gather.2.cloned.1.call-start = ((), (), s32[]{:S(2)}) async-start(), calls=%async_computation.3 | async-start | bytes 4718592 | tf_op jit(solution)/shard_map/all_gather | solution.py:21
  174.2 1.2 copy-start
  174.2 1.5 copy-start.1
  224.9 95.1 %all-to-all-start.2 = ((bf16[2,4,256,1024]{3,2,0,1:T(8,128)(2,1)}), bf16[2,4,256,1024]{3,2,0,1:T(8,128)(2,1)}, u32[]{:S(2)}, u32[]{:S(2)}) async-start(bf16[2,4,256,1024]{3,2,0,1:T(8,128)(2,1)} %select_bitcast_fusion), calls=%async_computation.2 | async-start | bytes 8388608 | tf_op jit(solution)/shard_map/all_to_all | solution.py:23
  231.8 11.0 %copy-start.2 = (bf16[1,1,2,1024,1024]{4,3,2,1,0:T(8,128)(2,1)S(1)}, bf16[1,1,2,1024,1024]{4,3,2,1,0:T(8,128)(2,1)}, u32[]{:S(2)}) copy-start(bf16[1,1,2,1024,1024]{4,3,2,1,0:T(8,128)(2,1)} %param.9) | copy-start | bytes 12582916
Sparse Core Ops, SparseCore 0:
  177.1 38.1 all-gather.1
where the time goes:
time: 338 us; the launch traced here: 332 us
  waiting for transfers between devices  194 us (57%)
  blocking collectives  51.6 us (15%)
  local copies, waits for them, and re-layouts  21.3 us (6%)
  matrix products  20.3 us (6%)
  other arithmetic  18.9 us (6%)
  between operations  15.5 us (5%)
  starting transfers between devices  10.2 us (3%)
    all_to_all x1, waiting for transfers between devices, outer_round(): lax.all_to_all(pieces, 'col', split_axis=1, concat_axis=1, tiled=True)  89.2 us
    all_to_all x1, waiting for transfers between devices, outer_round(): lax.all_to_all(chosen, 'col', split_axis=1, concat_axis=1, tiled=True)  66.2 us
    all_to_all x1, blocking collectives, outer_round(): lax.all_to_all(split, 'row', split_axis=2, concat_axis=2, tiled=True)  51.6 us
    all_gather x1, waiting for transfers between devices, outer_round(): lax.all_gather(outer_new.astype(jnp.bfloat16), 'row', axis=2, tiled=True)  38.3 us
    dot_general x2, matrix products, micro_step(): jnp.dot(normed, params_path[layer], preferred_element_type=jnp.float32)  20.3 us
  transfers between devices with their start and end apart: 3, of which 3 were waited for; matrix products, arithmetic and copies ran while one was open for 7% of the time, Pallas kernels for 0%

commit v1 on v0

v1 whole, which is shorter than its diff:
```python
import functools

import jax
import jax.numpy as jnp
from jax import lax
from jax.experimental import pallas as pl
from jax.experimental.pallas import tpu as pltpu
from jax.sharding import PartitionSpec as P

MESH = pl.DeviceIdType.MESH
BLOCK = 256
PARTS = 2
TILE = 192


def round_kernel(
    n_row, n_col, tokens, params, source, outer, moment, table, counts,
    path, outer_new, moment_new, hidden,
    weights, landed, own, z_out, z_in, chosen, state, normed,
    in_send, in_recv, z_send, z_recv, b_send, b_recv, ret_send, ret_recv, here_sem, *spread,
):
    row, col = lax.axis_index("row"), lax.axis_index("col")
    layers, width = params.shape[0], params.shape[2]
    part = width // PARTS
    blocks = part // BLOCK
    chunks = [(layer, p) for layer in range(layers) for p in range(PARTS)]
    n_chunks = len(chunks)

    barrier = pltpu.get_barrier_semaphore()
    for d in range(1, n_row):
        pl.semaphore_signal(barrier, inc=1, device_id=(lax.rem(row + d, n_row), col), device_id_type=MESH)
    for d in range(1, n_col):
        pl.semaphore_signal(barrier, inc=1, device_id=(row, lax.rem(col + d, n_col)), device_id_type=MESH)
    pl.semaphore_wait(barrier, n_row + n_col - 2)

    def cols(k):
        return pl.ds(chunks[k][1] * part, part)

    def in_copy(k, slot_of, to, peer):
        return pltpu.make_async_remote_copy(
            src_ref=source.at[chunks[k][0], :, to, :, cols(k)],
            dst_ref=landed.at[k, slot_of],
            send_sem=in_send.at[k, to],
            recv_sem=in_recv.at[k, slot_of],
            device_id=(peer, col),
            device_id_type=MESH,
        )

    def in_own(k):
        return pltpu.make_async_copy(source.at[chunks[k][0], :, row, :, cols(k)], landed.at[k, row], here_sem.at[0, k])

    def z_copy(k, slot_of, to):
        return pltpu.make_async_remote_copy(
            src_ref=z_out.at[k, to],
            dst_ref=z_in.at[k, slot_of],
            send_sem=z_send.at[k, to],
            recv_sem=z_recv.at[k, slot_of],
            device_id=(row, to),
            device_id_type=MESH,
        )

    def b_copy(k, slot_of, to):
        return pltpu.make_async_remote_copy(
            src_ref=spread[k].at[slot_of],
            dst_ref=spread[k].at[slot_of],
            send_sem=b_send.at[k, to],
            recv_sem=b_recv.at[k, slot_of],
            device_id=(row, to),
            device_id_type=MESH,
        )

    def ret_copy(k, slot_of, to):
        return pltpu.make_async_remote_copy(
            src_ref=chosen.at[k, to],
            dst_ref=path.at[chunks[k][0], :, slot_of, :, cols(k)],
            send_sem=ret_send.at[k, to],
            recv_sem=ret_recv.at[k, slot_of],
            device_id=(to, col),
            device_id_type=MESH,
        )

    def ret_own(k):
        return pltpu.make_async_copy(chosen.at[k, row], path.at[chunks[k][0], :, row, :, cols(k)], here_sem.at[1, k])

    def others(me, n):
        return [lax.rem(me + d, n) for d in range(1, n)]

    for k in range(n_chunks):
        in_own(k).start()
        for to in others(row, n_row):
            in_copy(k, row, to, to).start()

    def fill_weight(i, carry):
        mine = table[i, col]

        def add(at, total):
            r, c = at // n_col, at % n_col
            return total + jnp.where(table[r, c] == mine, counts[r, c], 0)

        total = lax.fori_loop(0, n_row * n_col, add, jnp.int32(0))
        shape = weights.shape[1:]
        weights[i] = jnp.full(shape, counts[i, col].astype(jnp.float32)) / jnp.full(shape, total.astype(jnp.float32))
        return carry

    lax.fori_loop(0, n_row, fill_weight, 0)

    def micro(start, size):
        rows = pl.ds(start, size)
        state[rows] = tokens[rows].astype(jnp.float32)
        for layer in range(layers):
            def norm(b, carry):
                few = pl.ds(pl.multiple_of(start + b * 16, 16), 16)
                value = state[few]
                scale = lax.rsqrt(jnp.mean(value * value, axis=-1, keepdims=True) + 1e-06)
                normed[few] = (value * scale).astype(jnp.bfloat16)
                return carry

            lax.fori_loop(0, size // 16, norm, 0)

            def mix(b, carry):
                at = pl.ds(pl.multiple_of(b * BLOCK, BLOCK), BLOCK)
                mixed = jnp.dot(normed[rows], params[layer, :, at], preferred_element_type=jnp.float32)
                state[rows, at] += 0.5 * mixed * (1.0 + lax.erf(mixed * (0.5**0.5)))
                return carry

            lax.fori_loop(0, width // BLOCK, mix, 0)
        hidden[rows] = state[rows].astype(jnp.bfloat16)

    def reduce(k):
        in_own(k).wait()
        for frm in others(row, n_row):
            in_copy(k, frm, frm, frm).wait_recv()
        for d in [*range(1, n_col), 0]:
            to = lax.rem(col + d, n_col)

            def block(b, carry, d=d, to=to):
                at = pl.ds(pl.multiple_of(b * BLOCK, BLOCK), BLOCK)
                sums = [jnp.zeros((landed.shape[3], BLOCK), jnp.float32) for _ in range(n_col)]
                for i in range(n_row):
                    term = (weights[i] * landed[k, i, to, :, at].astype(jnp.float32)).astype(jnp.bfloat16)
                    term = term.astype(jnp.float32)
                    module = table[i, col]
                    for m in range(n_col):
                        sums[m] += term * jnp.where(module == m, 1.0, 0.0).astype(jnp.float32)
                for m in range(n_col):
                    if d:
                        z_out[k, to, m, :, at] = sums[m].astype(jnp.bfloat16)
                    else:
                        own[k, m, :, at] = sums[m]
                return carry

            lax.fori_loop(0, blocks, block, 0)
            if d:
                z_copy(k, col, to).start()

    def update(k):
        layer, p = chunks[k]
        for frm in others(col, n_col):
            z_copy(k, frm, frm).wait_recv()

        def block(b, carry):
            at = pl.ds(pl.multiple_of(b * BLOCK, BLOCK), BLOCK)
            whole = pl.ds(pl.multiple_of(p * part + b * BLOCK, BLOCK), BLOCK)
            for m in range(n_col):
                average = own[k, m, :, at]
                for frm in others(col, n_col):
                    average += z_in[k, frm, m, :, at].astype(jnp.float32)
                old = outer[layer, m, :, whole]
                delta = old - average
                fresh = 0.9 * moment[layer, m, :, whole] + delta
                new = old - 0.7 * (delta + 0.9 * fresh)
                moment_new[layer, m, :, whole] = fresh
                outer_new[layer, m, :, whole] = new
                spread[k][col, m, :, at] = new.astype(jnp.bfloat16)
            return carry

        lax.fori_loop(0, blocks, block, 0)
        for to in others(col, n_col):
            b_copy(k, col, to).start()

    def give(k):
        for frm in others(col, n_col):
            b_copy(k, frm, frm).wait_recv()

        for d in [*range(1, n_row), 0]:
            to = lax.rem(row + d, n_row)
            module = table[to, col]

            def pick(c, carry, to=to, module=module):
                chosen[k, to, c] = spread[k][c, module]
                return carry

            lax.fori_loop(0, n_col, pick, 0)
            if d:
                ret_copy(k, row, to).start()
            else:
                ret_own(k).start()

    tiles = [(s, min(TILE, tokens.shape[0] - s)) for s in range(0, tokens.shape[0], TILE)]
    for step in range(max(n_chunks + 2, len(tiles))):
        if step < len(tiles):
            micro(*tiles[step])
        if 2 <= step < n_chunks + 2:
            give(step - 2)
        if 1 <= step < n_chunks + 1:
            update(step - 1)
        if step < n_chunks:
            reduce(step)

    for k in range(n_chunks):
        ret_own(k).wait()
        for at in others(row, n_row):
            ret_copy(k, at, at).wait_recv()
            in_copy(k, row, at, at).wait_send()
            ret_copy(k, row, at).wait_send()
        for at in others(col, n_col):
            z_copy(k, col, at).wait_send()
            b_copy(k, col, at).wait_send()


def with_kernel(tokens, params, outer, moment, table, counts):
    n_row, n_col = table.shape
    layers, width = params.shape[0], params.shape[-1]
    piece = outer.shape[2]
    part = width // PARTS
    n_chunks = layers * PARTS
    source = params.reshape(layers, n_col, n_row, piece, width)
    vmem = pl.BlockSpec(memory_space=pltpu.VMEM)
    smem = pl.BlockSpec(memory_space=pltpu.SMEM)
    hbm = pl.BlockSpec(memory_space=pl.ANY)
    n_tokens = tokens.shape[0]
    flops = 2 * layers * n_tokens * width * width
    return pl.pallas_call(
        functools.partial(round_kernel, n_row, n_col),
        out_shape=(
            jax.ShapeDtypeStruct(source.shape, jnp.bfloat16),
            jax.ShapeDtypeStruct(outer.shape, jnp.float32),
            jax.ShapeDtypeStruct(outer.shape, jnp.float32),
            jax.ShapeDtypeStruct(tokens.shape, jnp.bfloat16),
        ),
        in_specs=[vmem, vmem, hbm, vmem, vmem, smem, smem],
        out_specs=(hbm, vmem, vmem, vmem),
        scratch_shapes=[
            pltpu.VMEM((n_row, 1, BLOCK), jnp.float32),
            pltpu.VMEM((n_chunks, n_row, n_col, piece, part), jnp.bfloat16),
            pltpu.VMEM((n_chunks, n_col, piece, part), jnp.float32),
            pltpu.VMEM((n_chunks, n_col, n_col, piece, part), jnp.bfloat16),
            pltpu.VMEM((n_chunks, n_col, n_col, piece, part), jnp.bfloat16),
            pltpu.VMEM((n_chunks, n_row, n_col, piece, part), jnp.bfloat16),
            pltpu.VMEM((n_tokens, width), jnp.float32),
            pltpu.VMEM((n_tokens, width), jnp.bfloat16),
            pltpu.SemaphoreType.DMA((n_chunks, n_row)),
            pltpu.SemaphoreType.DMA((n_chunks, n_row)),
            pltpu.SemaphoreType.DMA((n_chunks, n_col)),
            pltpu.SemaphoreType.DMA((n_chunks, n_col)),
            pltpu.SemaphoreType.DMA((n_chunks, n_col)),
            pltpu.SemaphoreType.DMA((n_chunks, n_col)),
            pltpu.SemaphoreType.DMA((n_chunks, n_row)),
            pltpu.SemaphoreType.DMA((n_chunks, n_row)),
            pltpu.SemaphoreType.DMA((2, n_chunks)),
            *[pltpu.VMEM((n_col, n_col, piece, part), jnp.bfloat16) for _ in range(n_chunks)],
        ],
        compiler_params=pltpu.CompilerParams(
            collective_id=0, has_side_effects=True, vmem_limit_bytes=52 * 1024 * 1024
        ),
        cost_estimate=pl.CostEstimate(flops=flops, bytes_accessed=20 * 2**20, transcendentals=0),
    )(tokens, params, source, outer, moment, table, counts)


def pick_along(array, index, axis):
    parts = [lax.dynamic_index_in_dim(array, index[m], axis) for m in range(index.shape[0])]
    return jnp.concatenate(parts, axis=axis)


def with_collectives(tokens, params, outer, moment, table, counts):
    n_row, n_col = table.shape
    layers, width = params.shape[0], params.shape[-1]
    ids = jnp.arange(n_col, dtype=jnp.int32)
    matches = (table[:, :, None] == ids[None, None, :]).astype(jnp.float32)
    totals = jnp.sum(counts.astype(jnp.float32)[:, :, None] * matches, axis=(0, 1))
    my_row = lax.dynamic_index_in_dim(table, lax.axis_index("row"), 0, keepdims=False)
    count_row = lax.dynamic_index_in_dim(counts, lax.axis_index("row"), 0, keepdims=False)
    my_module = lax.dynamic_index_in_dim(my_row, lax.axis_index("col"), 0, keepdims=False)
    my_count = lax.dynamic_index_in_dim(count_row, lax.axis_index("col"), 0, keepdims=False)
    share = my_count.astype(jnp.float32) / jnp.sum(totals * (ids == my_module).astype(jnp.float32))
    inverse = jnp.sum(ids[:, None] * (my_row[:, None] == ids[None, :]).astype(jnp.int32), axis=0)
    scaled = (share * params.astype(jnp.float32)).astype(jnp.bfloat16)
    pieces = scaled.reshape(layers, n_col, width // n_col, width)
    arrived = lax.all_to_all(pieces, "col", split_axis=1, concat_axis=1, tiled=True)
    ordered = pick_along(arrived, inverse, 1)
    split = ordered.reshape(layers, n_col, n_row, width // (n_col * n_row), width)
    landed = lax.all_to_all(split, "row", split_axis=2, concat_axis=2, tiled=True)
    delta = outer - jnp.sum(landed.astype(jnp.float32), axis=2)
    moment_new = 0.9 * moment + delta
    outer_new = outer - 0.7 * (delta + 0.9 * moment_new)
    whole = lax.all_gather(outer_new.astype(jnp.bfloat16), "row", axis=2, tiled=True)
    chosen = pick_along(whole, my_row, 1)
    returned = lax.all_to_all(chosen, "col", split_axis=1, concat_axis=1, tiled=True)
    state = tokens.astype(jnp.float32)
    for layer in range(layers):
        scale = lax.rsqrt(jnp.mean(state * state, axis=-1, keepdims=True) + 1e-06)
        normed = (state * scale).astype(jnp.bfloat16)
        mixed = jnp.dot(normed, params[layer], preferred_element_type=jnp.float32)
        state = state + jax.nn.gelu(mixed, approximate=False)
    return returned, outer_new, moment_new, state.astype(jnp.bfloat16)


def on_device(tokens, local_params, outer_params, momentum, table, counts):
    n_col = table.shape[1]
    params = local_params[0, 0]
    layers, width = params.shape[0], params.shape[-1]
    outer = outer_params.reshape(layers, n_col, -1, width)
    moment = momentum.reshape(layers, n_col, -1, width)
    fits = outer.shape[2] % 16 == 0 and width % (PARTS * BLOCK) == 0 and tokens.shape[2] % 16 == 0
    run = with_kernel if fits else with_collectives
    returned, outer_new, moment_new, hidden = run(tokens[0, 0], params, outer, moment, table, counts)
    return (
        returned.reshape(local_params.shape),
        outer_new.reshape(outer_params.shape),
        moment_new.reshape(momentum.shape),
        hidden[None, None],
    )


def solution(mesh):
    return jax.shard_map(
        on_device,
        mesh=mesh,
        in_specs=(
            P("row", "col", None, None),
            P("row", "col", None, None, None),
            P(None, None, "col", "row", None, None),
            P(None, None, "col", "row", None, None),
            P(),
            P(),
        ),
        out_specs=(
            P("row", "col", None, None, None),
            P(None, None, "col", "row", None, None),
            P(None, None, "col", "row", None, None),
            P("row", "col", None, None),
        ),
        check_vma=False,
    )
```

time: 338 us -> 147 us (0.43); the launches traced: 332 us -> 147 us
  waiting for transfers between devices: 194 us -> 0 us
  Pallas kernels: 0 us -> 137 us
  blocking collectives: 51.6 us -> 0 us
  matrix products: 20.3 us -> 0 us
  other arithmetic: 18.9 us -> 0 us
  between operations: 15.5 us -> 0.65 us
  local copies, waits for them, and re-layouts: 21.3 us -> 9.31 us
  starting transfers between devices: 10.2 us -> 0 us
    all_to_all x2 -> x0, waiting for transfers between devices: 155 us -> none  [the longest x1 89.2 us: outer_round(): lax.all_to_all(pieces, 'col', split_axis=1, concat_axis=1, tiled=True)]
    pallas_call x0 -> x1, Pallas kernels: none -> 137 us  [with_kernel(): pl.pallas_call(functools.partial(round_kernel, n_row, n_col), out_shape=(...]
    all_to_all x1 -> x0, blocking collectives: 51.6 us -> none  [outer_round(): lax.all_to_all(split, 'row', split_axis=2, concat_axis=2, tiled=True)]
    all_gather x1 -> x0, waiting for transfers between devices: 38.3 us -> none  [outer_round(): lax.all_gather(outer_new.astype(jnp.bfloat16), 'row', axis=2, tiled=True)]
    dot_general x2 -> x0, matrix products: 20.3 us -> none  [micro_step(): jnp.dot(normed, params_path[layer], preferred_element_type=jnp.float32)]
    all_to_all x2 -> x0, starting transfers between devices: 10.2 us -> none  [the longest x1 5.12 us: outer_round(): lax.all_to_all(pieces, 'col', split_axis=1, concat_axis=1, tiled=True)]
    gather x2 -> x0, local copies, waits for them, and re-layouts: 10 us -> none  [the longest x1 5.01 us: outer_round(): chosen = jnp.take(whole, my_row, axis=1)]
    unnamed x8 -> x10, local copies, waits for them, and re-layouts: 0.67 us -> 9.31 us
  transfers between devices with their start and end apart: 3 -> 0, of which waited for: 3 -> 0; matrix products, arithmetic and copies ran while one was open for 7% -> 0% of each run, Pallas kernels for 0% -> 0%
where the time goes in v1:
time: 147 us
  Pallas kernels  137 us (93%)
  local copies, waits for them, and re-layouts  9.31 us (6%)
    pallas_call x1, Pallas kernels, with_kernel(): pl.pallas_call(functools.partial(round_kernel, n_row, n_col), out_shape=(...  137 us
    unnamed x10, local copies, waits for them, and re-layouts  9.31 us

profile of v1, /device:TPU:15, one launch (start us, length us, event | category | flops | bytes accessed | tf_op | source)
XLA Modules:
  0.0 147.0 jit_solution(13865327722790316332)
XLA Ops:
  0.6 0.8 copy.10.table
  1.4 0.8 copy.11.counts
  2.1 137.1 %shard_map.93 = (bf16[2,4,8,32,1024]{4,3,2,1,0:T(8,128)(2,1)}, f32[2,4,32,1024]{3,2,1,0:T(8,128)S(1)}, f32[2,4,32,1024]{3,2,1,0:T(8,128)}, bf16[736,1024]{1,0:T(8,128)(2,1)}) custom-call(bf16[736,1024]{1,0:T(8,128)(2,1)} %bitcast.17, bf16[2,1024,1024]{2,1,0:T(8,128)(2,1)} %bitcast.14, bf16[2,4,8,32,1024]{4,3,2,1,0:T(8,128)(2,1)} %bitcast.15, ...), custom_call_target="tpu_custom_call" | custom-call | flops 3087007744 | bytes 20971520 | tf_op jit(solution)/shard_map/pallas_call | solution.py:233
  139.2 0.0 copy-start.1
  139.2 4.7 %copy.18 = bf16[1,1,2,1024,1024]{4,3,2,1,0:T(8,128)(2,1)} copy(bf16[1,1,2,1024,1024]{4,3,2,1,0:T(8,128)(2,1)} %bitcast.16) | data formatting | bytes 8388608
  143.9 0.0 copy-start
  144.0 1.0 copy.19
  144.9 0.0 copy-done.1
  144.9 1.0 copy.20
  145.9 0.0 copy-done
  145.9 1.1 copy.21
Async XLA Ops:
  139.2 5.7 %copy-start.1 = (f32[2,4,32,1024]{3,2,1,0:T(8,128)S(1)}, f32[2,4,32,1024]{3,2,1,0:T(8,128)}, u32[]{:S(2)}) copy-start(f32[2,4,32,1024]{3,2,1,0:T(8,128)} %get-tuple-element.10) | copy-start | bytes 3145732
  143.9 1.9 %copy-start = (bf16[736,1024]{1,0:T(8,128)(2,1)S(1)}, bf16[736,1024]{1,0:T(8,128)(2,1)}, u32[]{:S(2)}) copy-start(bf16[736,1024]{1,0:T(8,128)(2,1)} %get-tuple-element.11) | copy-start | bytes 4521988

commit v2 on v1

--- a/solution.py
+++ b/solution.py
@@ -14,10 +14,12 @@
 
 
 def round_kernel(
-    n_row, n_col, tokens, params, source, outer, moment, table, counts,
-    path, outer_new, moment_new, hidden,
-    weights, landed, own, z_out, z_in, chosen, state, normed,
-    in_send, in_recv, z_send, z_recv, b_send, b_recv, ret_send, ret_recv, here_sem, *spread,
+    n_row, n_col, tokens_in, params_in, source, outer_in, moment_in, table, counts,
+    path, outer_out, moment_out, hidden_out,
+    tokens, params, outer, moment, outer_new, moment_new, hidden,
+    weights, landed, own, pair_out, pair_in, z_out, z_in, chosen, state, normed,
+    in_send, in_recv, pair_send, pair_recv, z_send, z_recv, b_send, b_recv, f_send, f_recv,
+    ret_send, ret_recv, here_sem, load_sem, store_sem, *spread,
 ):
     row, col = lax.axis_index("row"), lax.axis_index("col")
     layers, width = params.shape[0], params.shape[2]
@@ -25,6 +27,9 @@
     blocks = part // BLOCK
     chunks = [(layer, p) for layer in range(layers) for p in range(PARTS)]
     n_chunks = len(chunks)
+    half = n_col // 2
+    fresh_own, near, far = (spread[i * n_chunks : (i + 1) * n_chunks] for i in range(3))
+    pair = col + 1 - 2 * lax.rem(col, 2)
 
     barrier = pltpu.get_barrier_semaphore()
     for d in range(1, n_row):
@@ -36,66 +41,65 @@
     def cols(k):
         return pl.ds(chunks[k][1] * part, part)
 
-    def in_copy(k, slot_of, to, peer):
+    def remote(src, dst, send, recv, to):
         return pltpu.make_async_remote_copy(
-            src_ref=source.at[chunks[k][0], :, to, :, cols(k)],
-            dst_ref=landed.at[k, slot_of],
-            send_sem=in_send.at[k, to],
-            recv_sem=in_recv.at[k, slot_of],
-            device_id=(peer, col),
-            device_id_type=MESH,
+            src_ref=src, dst_ref=dst, send_sem=send, recv_sem=recv, device_id=to, device_id_type=MESH
         )
+
+    def in_copy(k, slot, to):
+        src = source.at[chunks[k][0], :, to, :, cols(k)]
+        return remote(src, landed.at[k, slot], in_send.at[k, to], in_recv.at[k, slot], (to, col))
 
     def in_own(k):
         return pltpu.make_async_copy(source.at[chunks[k][0], :, row, :, cols(k)], landed.at[k, row], here_sem.at[0, k])
 
-    def z_copy(k, slot_of, to):
-        return pltpu.make_async_remote_copy(
-            src_ref=z_out.at[k, to],
-            dst_ref=z_in.at[k, slot_of],
-            send_sem=z_send.at[k, to],
-            recv_sem=z_recv.at[k, slot_of],
-            device_id=(row, to),
-            device_id_type=MESH,
-        )
-
-    def b_copy(k, slot_of, to):
-        return pltpu.make_async_remote_copy(
-            src_ref=spread[k].at[slot_of],
-            dst_ref=spread[k].at[slot_of],
-            send_sem=b_send.at[k, to],
-            recv_sem=b_recv.at[k, slot_of],
-            device_id=(row, to),
-            device_id_type=MESH,
-        )
-
-    def ret_copy(k, slot_of, to):
-        return pltpu.make_async_remote_copy(
-            src_ref=chosen.at[k, to],
-            dst_ref=path.at[chunks[k][0], :, slot_of, :, cols(k)],
-            send_sem=ret_send.at[k, to],
-            recv_sem=ret_recv.at[k, slot_of],
-            device_id=(to, col),
-            device_id_type=MESH,
-        )
+    def pair_copy(k):
+        return remote(pair_out.at[k], pair_in.at[k], pair_send.at[k], pair_recv.at[k], (row, pair))
+
+    def ahead(d):
+        return (row, lax.rem(col + 2 * d, n_col))
+
+    def z_copy(k, d):
+        return remote(z_out.at[k, d - 1], z_in.at[k, d - 1], z_send.at[k, d], z_recv.at[k, d], ahead(d))
+
+    def b_copy(k, d):
+        return remote(fresh_own[k], near[k].at[d - 1], b_send.at[k, d], b_recv.at[k, d], ahead(d))
+
+    def f_copy(k, d):
+        block = near[k].at[d - 1] if d else fresh_own[k]
+        return remote(block, far[k].at[d], f_send.at[k, d], f_recv.at[k, d], (row, pair))
+
+    def ret_copy(k, slot, to):
+        dst = path.at[chunks[k][0], :, slot, :, cols(k)]
+        return remote(chosen.at[k, to], dst, ret_send.at[k, to], ret_recv.at[k, slot], (to, col))
 
     def ret_own(k):
         return pltpu.make_async_copy(chosen.at[k, row], path.at[chunks[k][0], :, row, :, cols(k)], here_sem.at[1, k])
 
     def others(me, n):
         return [lax.rem(me + d, n) for d in range(1, n)]
+
+    loads = [
+        pltpu.make_async_copy(src, dst, load_sem.at[i])
+        for i, (src, dst) in enumerate(
+            [(tokens_in, tokens), (params_in, params), (outer_in, outer), (moment_in, moment)]
+        )
+    ]
 
     for k in range(n_chunks):
         in_own(k).start()
         for to in others(row, n_row):
-            in_copy(k, row, to, to).start()
+            in_copy(k, row, to).start()
+        if k == 0:
+            for load in loads:
+                load.start()
 
     def fill_weight(i, carry):
-        mine = table[i, col]
+        module = table[i, col]
 
         def add(at, total):
             r, c = at // n_col, at % n_col
-            return total + jnp.where(table[r, c] == mine, counts[r, c], 0)
+            return total + jnp.where(table[r, c] == module, counts[r, c], 0)
 
         total = lax.fori_loop(0, n_row * n_col, add, jnp.int32(0))
         shape = weights.shape[1:]
@@ -129,93 +133,143 @@
     def reduce(k):
         in_own(k).wait()
         for frm in others(row, n_row):
-            in_copy(k, frm, frm, frm).wait_recv()
-        for d in [*range(1, n_col), 0]:
-            to = lax.rem(col + d, n_col)
-
-            def block(b, carry, d=d, to=to):
+            in_copy(k, frm, frm).wait_recv()
+
+        def sums_of(to, at):
+            sums = [jnp.zeros((landed.shape[3], BLOCK), jnp.float32) for _ in range(n_col)]
+            for i in range(n_row):
+                term = (weights[i] * landed[k, i, to, :, at].astype(jnp.float32)).astype(jnp.bfloat16)
+                term = term.astype(jnp.float32)
+                module = table[i, col]
+                for m in range(n_col):
+                    sums[m] += term * jnp.where(module == m, 1.0, 0.0).astype(jnp.float32)
+            return sums
+
+        for d in range(half):
+
+            def away(b, carry, d=d):
                 at = pl.ds(pl.multiple_of(b * BLOCK, BLOCK), BLOCK)
-                sums = [jnp.zeros((landed.shape[3], BLOCK), jnp.float32) for _ in range(n_col)]
-                for i in range(n_row):
-                    term = (weights[i] * landed[k, i, to, :, at].astype(jnp.float32)).astype(jnp.bfloat16)
-                    term = term.astype(jnp.float32)
-                    module = table[i, col]
-                    for m in range(n_col):
-                        sums[m] += term * jnp.where(module == m, 1.0, 0.0).astype(jnp.float32)
-                for m in range(n_col):
-                    if d:
-                        z_out[k, to, m, :, at] = sums[m].astype(jnp.bfloat16)
-                    else:
-                        own[k, m, :, at] = sums[m]
+                for m, value in enumerate(sums_of(lax.rem(pair + 2 * d, n_col), at)):
+                    pair_out[k, d, m, :, at] = value.astype(jnp.bfloat16)
                 return carry
 
-            lax.fori_loop(0, blocks, block, 0)
-            if d:
-                z_copy(k, col, to).start()
+            lax.fori_loop(0, blocks, away, 0)
+        pair_copy(k).start()
+
+        for d in range(half):
+
+            def kept(b, carry, d=d):
+                at = pl.ds(pl.multiple_of(b * BLOCK, BLOCK), BLOCK)
+                for m, value in enumerate(sums_of(lax.rem(col + 2 * d, n_col), at)):
+                    own[k, d, m, :, at] = value
+                return carry
+
+            lax.fori_loop(0, blocks, kept, 0)
+
+    def halfway(k):
+        pair_copy(k).wait_recv()
+        for d in range(1, half):
+
+            def block(m, carry, d=d):
+                z_out[k, d - 1, m] = (own[k, d, m] + pair_in[k, d, m].astype(jnp.float32)).astype(jnp.bfloat16)
+                return carry
+
+            lax.fori_loop(0, n_col, block, 0)
+            z_copy(k, d).start()
 
     def update(k):
         layer, p = chunks[k]
-        for frm in others(col, n_col):
-            z_copy(k, frm, frm).wait_recv()
+        for d in range(1, half):
+            z_copy(k, d).wait_recv()
 
         def block(b, carry):
             at = pl.ds(pl.multiple_of(b * BLOCK, BLOCK), BLOCK)
             whole = pl.ds(pl.multiple_of(p * part + b * BLOCK, BLOCK), BLOCK)
             for m in range(n_col):
-                average = own[k, m, :, at]
-                for frm in others(col, n_col):
-                    average += z_in[k, frm, m, :, at].astype(jnp.float32)
+                average = own[k, 0, m, :, at] + pair_in[k, 0, m, :, at].astype(jnp.float32)
+                for d in range(1, half):
+                    average += z_in[k, d - 1, m, :, at].astype(jnp.float32)
                 old = outer[layer, m, :, whole]
                 delta = old - average
                 fresh = 0.9 * moment[layer, m, :, whole] + delta
                 new = old - 0.7 * (delta + 0.9 * fresh)
                 moment_new[layer, m, :, whole] = fresh
                 outer_new[layer, m, :, whole] = new
-                spread[k][col, m, :, at] = new.astype(jnp.bfloat16)
+                fresh_own[k][m, :, at] = new.astype(jnp.bfloat16)
             return carry
 
         lax.fori_loop(0, blocks, block, 0)
-        for to in others(col, n_col):
-            b_copy(k, col, to).start()
+        for d in range(1, half):
+            b_copy(k, d).start()
+        f_copy(k, 0).start()
+
+    def forward(k):
+        for d in range(1, half):
+            b_copy(k, d).wait_recv()
+            f_copy(k, d).start()
 
     def give(k):
-        for frm in others(col, n_col):
-            b_copy(k, frm, frm).wait_recv()
+        for h in range(half):
+            f_copy(k, h).wait_recv()
 
         for d in [*range(1, n_row), 0]:
             to = lax.rem(row + d, n_row)
             module = table[to, col]
-
-            def pick(c, carry, to=to, module=module):
-                chosen[k, to, c] = spread[k][c, module]
-                return carry
-
-            lax.fori_loop(0, n_col, pick, 0)
+            for back in range(half):
+                apart = n_col - 2 * back
+                chosen[k, to, lax.rem(col + apart, n_col)] = near[k][back - 1, module] if back else fresh_own[k][module]
+                chosen[k, to, lax.rem(pair + apart, n_col)] = far[k][back, module]
             if d:
                 ret_copy(k, row, to).start()
             else:
                 ret_own(k).start()
 
+    stores = [
+        pltpu.make_async_copy(src, dst, store_sem.at[i])
+        for i, (src, dst) in enumerate([(outer_new, outer_out), (moment_new, moment_out), (hidden, hidden_out)])
+    ]
     tiles = [(s, min(TILE, tokens.shape[0] - s)) for s in range(0, tokens.shape[0], TILE)]
     for step in range(max(n_chunks + 2, len(tiles))):
-        if step < len(tiles):
-            micro(*tiles[step])
+        if step < n_chunks:
+            reduce(step)
+        if 1 <= step < n_chunks + 1:
+            if step == 1:
+                loads[2].wait()
+                loads[3].wait()
+            update(step - 1)
+            if step == n_chunks:
+                stores[0].start()
+                stores[1].start()
         if 2 <= step < n_chunks + 2:
             give(step - 2)
+        if step < len(tiles):
+            if step == 0:
+                loads[0].wait()
+                loads[1].wait()
+            micro(*tiles[step])
+            if step == len(tiles) - 1:
+                stores[2].start()
+        if step < n_chunks:
+            halfway(step)
         if 1 <= step < n_chunks + 1:
-            update(step - 1)
-        if step < n_chunks:
-            reduce(step)
+            forward(step - 1)
 
     for k in range(n_chunks):
+        pair_copy(k).wait_send()
+        for d in range(half):
+            if d:
+                z_copy(k, d).wait_send()
+                b_copy(k, d).wait_send()
+            f_copy(k, d).wait_send()
         ret_own(k).wait()
         for at in others(row, n_row):
+            in_copy(k, row, at).wait_send()
+            ret_copy(k, row, at).wait_send()
+    for k in range(n_chunks):
+        for at in others(row, n_row):
             ret_copy(k, at, at).wait_recv()
-            in_copy(k, row, at, at).wait_send()
-            ret_copy(k, row, at).wait_send()
-        for at in others(col, n_col):
-            z_copy(k, col, at).wait_send()
-            b_copy(k, col, at).wait_send()
+    for store in stores:
+        store.wait()
 
 
 def with_kernel(tokens, params, outer, moment, table, counts):
@@ -224,12 +278,15 @@
     piece = outer.shape[2]
     part = width // PARTS
     n_chunks = layers * PARTS
+    half = n_col // 2
     source = params.reshape(layers, n_col, n_row, piece, width)
-    vmem = pl.BlockSpec(memory_space=pltpu.VMEM)
     smem = pl.BlockSpec(memory_space=pltpu.SMEM)
     hbm = pl.BlockSpec(memory_space=pl.ANY)
     n_tokens = tokens.shape[0]
     flops = 2 * layers * n_tokens * width * width
+    by_row = pltpu.SemaphoreType.DMA((n_chunks, n_row))
+    by_half = pltpu.SemaphoreType.DMA((n_chunks, half))
+    by_chunk = pltpu.SemaphoreType.DMA((n_chunks,))
     return pl.pallas_call(
         functools.partial(round_kernel, n_row, n_col),
         out_shape=(
@@ -238,27 +295,33 @@
             jax.ShapeDtypeStruct(outer.shape, jnp.float32),
             jax.ShapeDtypeStruct(tokens.shape, jnp.bfloat16),
         ),
-        in_specs=[vmem, vmem, hbm, vmem, vmem, smem, smem],
-        out_specs=(hbm, vmem, vmem, vmem),
+        in_specs=[hbm, hbm, hbm, hbm, hbm, smem, smem],
+        out_specs=(hbm, hbm, hbm, hbm),
         scratch_shapes=[
+            pltpu.VMEM(tokens.shape, jnp.bfloat16),
+            pltpu.VMEM(params.shape, jnp.bfloat16),
+            pltpu.VMEM(outer.shape, jnp.float32),
+            pltpu.VMEM(outer.shape, jnp.float32),
+            pltpu.VMEM(outer.shape, jnp.float32),
+            pltpu.VMEM(outer.shape, jnp.float32),
+            pltpu.VMEM(tokens.shape, jnp.bfloat16),
             pltpu.VMEM((n_row, 1, BLOCK), jnp.float32),
             pltpu.VMEM((n_chunks, n_row, n_col, piece, part), jnp.bfloat16),
-            pltpu.VMEM((n_chunks, n_col, piece, part), jnp.float32),
-            pltpu.VMEM((n_chunks, n_col, n_col, piece, part), jnp.bfloat16),
-            pltpu.VMEM((n_chunks, n_col, n_col, piece, part), jnp.bfloat16),
+            pltpu.VMEM((n_chunks, half, n_col, piece, part), jnp.float32),
+            pltpu.VMEM((n_chunks, half, n_col, piece, part), jnp.bfloat16),
+            pltpu.VMEM((n_chunks, half, n_col, piece, part), jnp.bfloat16),
+            pltpu.VMEM((n_chunks, half, n_col, piece, part), jnp.bfloat16),
+            pltpu.VMEM((n_chunks, half, n_col, piece, part), jnp.bfloat16),
             pltpu.VMEM((n_chunks, n_row, n_col, piece, part), jnp.bfloat16),
             pltpu.VMEM((n_tokens, width), jnp.float32),
             pltpu.VMEM((n_tokens, width), jnp.bfloat16),
-            pltpu.SemaphoreType.DMA((n_chunks, n_row)),
-            pltpu.SemaphoreType.DMA((n_chunks, n_row)),
-            pltpu.SemaphoreType.DMA((n_chunks, n_col)),
-            pltpu.SemaphoreType.DMA((n_chunks, n_col)),
-            pltpu.SemaphoreType.DMA((n_chunks, n_col)),
-            pltpu.SemaphoreType.DMA((n_chunks, n_col)),
-            pltpu.SemaphoreType.DMA((n_chunks, n_row)),
-            pltpu.SemaphoreType.DMA((n_chunks, n_row)),
+            by_row, by_row, by_chunk, by_chunk, by_half, by_half, by_half, by_half, by_half, by_half, by_row, by_row,
             pltpu.SemaphoreType.DMA((2, n_chunks)),
-            *[pltpu.VMEM((n_col, n_col, piece, part), jnp.bfloat16) for _ in range(n_chunks)],
+            pltpu.SemaphoreType.DMA((4,)),
+            pltpu.SemaphoreType.DMA((3,)),
+            *[pltpu.VMEM((n_col, piece, part), jnp.bfloat16) for _ in range(n_chunks)],
+            *[pltpu.VMEM((max(half - 1, 1), n_col, piece, part), jnp.bfloat16) for _ in range(n_chunks)],
+            *[pltpu.VMEM((half, n_col, piece, part), jnp.bfloat16) for _ in range(n_chunks)],
         ],
         compiler_params=pltpu.CompilerParams(
             collective_id=0, has_side_effects=True, vmem_limit_bytes=52 * 1024 * 1024
@@ -311,7 +374,7 @@
     layers, width = params.shape[0], params.shape[-1]
     outer = outer_params.reshape(layers, n_col, -1, width)
     moment = momentum.reshape(layers, n_col, -1, width)
-    fits = outer.shape[2] % 16 == 0 and width % (PARTS * BLOCK) == 0 and tokens.shape[2] % 16 == 0
+    fits = n_col % 2 == 0 and outer.shape[2] % 16 == 0 and width % (PARTS * BLOCK) == 0 and tokens.shape[2] % 16 == 0
     run = with_kernel if fits else with_collectives
     returned, outer_new, moment_new, hidden = run(tokens[0, 0], params, outer, moment, table, counts)
     return (

time: 147 us -> 120 us (0.82); the launches traced: 147 us -> 118 us
  Pallas kernels: 137 us -> 109 us
    pallas_call x1, Pallas kernels: 137 us -> 109 us  [with_kernel(): pl.pallas_call(functools.partial(round_kernel, n_row, n_col), out_shape=(...]
where the time goes in v2:
time: 120 us; the launch traced here: 118 us
  Pallas kernels  109 us (91%)
  local copies, waits for them, and re-layouts  9.31 us (8%)
    pallas_call x1, Pallas kernels, with_kernel(): pl.pallas_call(functools.partial(round_kernel, n_row, n_col), out_shape=(...  109 us
    unnamed x10, local copies, waits for them, and re-layouts  9.31 us

profile of v2, /device:TPU:15, one launch (start us, length us, event | category | flops | bytes accessed | tf_op | source)
XLA Modules:
  0.0 118.5 jit_solution(13377485462521108077)
XLA Ops:
  0.6 0.8 copy.10.table
  1.4 0.8 copy.11.counts
  2.1 108.5 %shard_map.93 = (bf16[2,4,8,32,1024]{4,3,2,1,0:T(8,128)(2,1)}, f32[2,4,32,1024]{3,2,1,0:T(8,128)S(1)}, f32[2,4,32,1024]{3,2,1,0:T(8,128)}, bf16[736,1024]{1,0:T(8,128)(2,1)}) custom-call(bf16[736,1024]{1,0:T(8,128)(2,1)} %bitcast.17, bf16[2,1024,1024]{2,1,0:T(8,128)(2,1)} %bitcast.14, bf16[2,4,8,32,1024]{4,3,2,1,0:T(8,128)(2,1)} %bitcast.15, ...), custom_call_target="tpu_custom_call" | custom-call | flops 3087007744 | bytes 20971520 | tf_op jit(solution)/shard_map/pallas_call | solution.py:290
  110.7 0.0 copy-start.1
  110.7 4.7 %copy.18 = bf16[1,1,2,1024,1024]{4,3,2,1,0:T(8,128)(2,1)} copy(bf16[1,1,2,1024,1024]{4,3,2,1,0:T(8,128)(2,1)} %bitcast.16) | data formatting | bytes 8388608
  115.4 0.0 copy-start
  115.4 1.0 copy.19
  116.4 0.0 copy-done.1
  116.4 1.0 copy.20
  117.3 0.0 copy-done
  117.3 1.1 copy.21
Async XLA Ops:
  110.7 5.7 %copy-start.1 = (f32[2,4,32,1024]{3,2,1,0:T(8,128)S(1)}, f32[2,4,32,1024]{3,2,1,0:T(8,128)}, u32[]{:S(2)}) copy-start(f32[2,4,32,1024]{3,2,1,0:T(8,128)} %get-tuple-element.10) | copy-start | bytes 3145732
  115.4 1.9 %copy-start = (bf16[736,1024]{1,0:T(8,128)(2,1)S(1)}, bf16[736,1024]{1,0:T(8,128)(2,1)}, u32[]{:S(2)}) copy-start(bf16[736,1024]{1,0:T(8,128)(2,1)} %get-tuple-element.11) | copy-start | bytes 4521988
